TPU v7x, 32 devices: a whole 2x2x4 slice. The times are simulated.
32 devices in a mesh: groups: 2 (over y), wide: 8 (over z, x), tp: 2 (over core).
Axes of the slice: x: 2, y: 2, z: 4, core: 2. Of those that a mesh axis runs over, the one named last changes fastest.
Arguments:
- pre_codes: bfloat16 [64, 4, 4, 2, 512], P(('groups', 'wide'), None, 'tp'), parts along dimension 0, may hold values from -6 to 6
- pre_scales: bfloat16 [64, 4, 4, 2, 4], P(('groups', 'wide'), None, 'tp'), parts along dimension 0, may hold values from 0.099609375 to 1
- req_dest: int32 [64], P(('groups', 'wide')), parts along dimension 0, may hold values from 0 to 7, as said below
- req_blocks: int32 [64], P(('groups', 'wide')), parts along dimension 0, may hold values from 1 to 4, as said below
- res_codes: bfloat16 [128, 64, 2, 512], P(('groups', 'wide'), None, None, 'tp'), parts along dimension 0, may hold values from -6 to 6
- res_scales: bfloat16 [128, 64, 2, 4], P(('groups', 'wide'), None, None, 'tp'), parts along dimension 0, may hold values from 0.099609375 to 1
- res_len: int32 [128], P(('groups', 'wide')), parts along dimension 0, may hold values from 1 to 64, as said below
- res_query: bfloat16 [128, 2, 8192], P(('groups', 'wide'), None, 'tp'), parts along dimension 0, may hold values from -128 to 128
- res_new: bfloat16 [128, 2, 2, 512], P(('groups', 'wide'), None, None, 'tp'), parts along dimension 0, may hold values from -6 to 6
- arr_query: bfloat16 [96, 2, 8192], P(('groups', 'wide'), None, 'tp'), parts along dimension 0, may hold values from -128 to 128
- arr_new: bfloat16 [96, 2, 2, 512], P(('groups', 'wide'), None, None, 'tp'), parts along dimension 0, may hold values from -6 to 6
Outputs:
- res_out: bfloat16 [128, 2, 8192], P(('groups', 'wide'), None, 'tp'), parts along dimension 0
- arr_out: bfloat16 [96, 2, 8192], P(('groups', 'wide'), None, 'tp'), parts along dimension 0
There are 2 independent parts, one for each index of `groups`. A program takes and returns all parts, laid end to end along the dimension named above; each array names one. Nothing has to cross between parts.
Inputs may be any that keep to these rules, and one draw needn't show every extreme that they name: `req_dest`: each prefill instance sends at most one request to one decode instance; each decode instance receives at least 2 and at most 6 requests, and some decode instance receives 6 in every draw. For every even r, request r of each prefill instance goes to the instance a fixed distance away along the axis, the same distance for all prefill instances, and request r + 1 to the instance at one of two further such distances. `req_blocks`: some request holds 4 blocks in every draw. `res_len`: some resident request has 64 tokens in every draw.
All inputs are finite; a program needn't handle non-finite values.
Results may differ from a plain program's by a relative error of at most 0.0032.
Values may be sent and summed in bfloat16 or wider, within the bound.
No kernel may reach another device: no remote copies, remote signals or barrier semaphores. Data moves between devices by JAX's collectives and lax.ppermute only.
A program may use at most 64 MiB of HBM per device.

v0:
```python
import functools
import math

import jax
import jax.numpy as jnp
from jax import lax
from jax.experimental import pallas as pl
from jax.experimental.pallas import tpu as pltpu
from jax.sharding import PartitionSpec as P

KVH = 4
HD = 128
HQ = 64
GROUP = HQ // KVH
STEPS = 2

NEGATIVE = -1e30
EMPTY = 1024.0
SCORE_SCALE = 1.0 / math.sqrt(HD)

BF16 = jnp.bfloat16
F32 = jnp.float32


def iota(shape, axis):
    return lax.broadcasted_iota(jnp.int32, shape, axis)


def over(x, n):
    return jnp.right_shift(x, n.bit_length() - 1) if n & (n - 1) == 0 else x // n


def mod(x, n):
    return jnp.bitwise_and(x, n - 1) if n & (n - 1) == 0 else x % n


def dot_nt(a, b):
    return lax.dot_general(a, b, (((1,), (1,)), ((), ())), preferred_element_type=F32)


def dot_nn(a, b):
    return lax.dot_general(a, b, (((1,), (0,)), ((), ())), preferred_element_type=F32)


def top_of(*parts):
    return functools.reduce(jnp.maximum, [jnp.max(p, axis=1, keepdims=True) for p in parts])


def sum_of(*parts):
    return functools.reduce(jnp.add, [jnp.sum(p, axis=1, keepdims=True) for p in parts])


def to_values(weights):
    tiles = [pltpu.roll(weights[:, c : c + HD], 1, 1) for c in range(0, weights.shape[1], HD)]
    return jnp.concatenate(tiles, axis=1).astype(BF16)


def values_up(rows):
    return pltpu.roll(rows.astype(F32), rows.shape[0] - 1, 0).astype(BF16)


def pack_kernel(
    tp, order, heads, block_rows, dest_hbm, blocks_hbm, codes_hbm, scales_hbm, send_ref,
    dest_ref, blocks_ref, codes_ref, scales_ref, sems,
):
    requests, all_rows = codes_ref.shape[:2]
    pairs = [
        (codes_hbm.at[: requests // 2], codes_ref.at[: requests // 2]),
        (codes_hbm.at[requests // 2 :], codes_ref.at[requests // 2 :]),
        (scales_hbm, scales_ref), (dest_hbm, dest_ref), (blocks_hbm, blocks_ref),
    ]
    copies = [pltpu.make_async_copy(a, b, sems.at[i]) for i, (a, b) in enumerate(pairs)]
    for copy in copies:
        copy.start()
    rows = all_rows // heads
    per_core = heads // tp
    send_ref[...] = jnp.full(send_ref.shape, EMPTY, BF16)
    row_block = over(iota((rows, HD), 0), block_rows)
    to_row = iota((all_rows, all_rows), 0)
    from_row = iota((all_rows, all_rows), 1)
    source = over(mod(to_row, rows), 2) * (2 * heads) + over(to_row, rows) * 2 + mod(to_row, 2)
    by_head = jnp.where(from_row == source, 1.0, 0.0).astype(BF16)
    for copy in copies:
        copy.wait()

    def place(r):
        there = dest_ref[r]
        spots = [there * tp + t for t in range(tp)]
        if order is not None:
            for t in range(tp):
                at = {core // tp: p for p, core in enumerate(order) if core % tp == t}
                spots[t] = functools.reduce(
                    jnp.add, [jnp.where(there == w, p, 0) for w, p in at.items()]
                )
        held = row_block < blocks_ref[r]
        codes = dot_nn(by_head, codes_ref[r])
        scales = scales_ref[r].astype(F32)
        for j in range(heads):
            values = codes[j * rows : (j + 1) * rows] * scales[:, j : j + 1]
            values = jnp.where(held, values, EMPTY).astype(BF16)
            send_ref[spots[j // per_core], j % per_core] = values

    if requests <= 8:
        for r in range(requests):
            place(r)
    else:
        lax.fori_loop(0, requests, lambda r, c: (place(r), c)[1], 0)


def resident_kernel(
    len_ref, codes_hbm, scales_ref, query_ref, new_ref, out_ref, codes_ref, sem
):
    fetch = pltpu.make_async_copy(codes_hbm, codes_ref, sem)
    fetch.start()
    slots, rows = codes_ref.shape[:2]
    heads = scales_ref.shape[2]
    tokens = rows // (2 * heads)
    queries = query_ref.shape[1]
    new_rows = new_ref.shape[0]

    row = iota((rows, HD), 0)
    source = (mod(row, 2) * heads + mod(over(row, 2), heads)) * tokens + over(row, 2 * heads)
    lane = iota((rows, HD), 1)
    spread = jnp.concatenate(
        [jnp.where(source == lane + c, 1.0, 0.0).astype(BF16) for c in range(0, rows, HD)],
        axis=1,
    )
    flat = jnp.concatenate(
        [scales_ref[:, p, h] for p in range(2) for h in range(heads)], axis=1
    )
    columns = dot_nt(spread, flat).astype(BF16)

    col = iota((queries, rows), 1)
    row_head = over(iota((queries, rows), 0), queries // heads)
    is_key = (mod(col, 2) == 0) & (mod(over(col, 2), heads) == row_head)
    col_token = jnp.where(is_key, over(col, 2 * heads), tokens)

    new_col = iota((queries, new_rows), 1)
    new_row = iota((queries, new_rows), 0)
    new_ok = (
        (mod(new_col, 2) == 0)
        & (mod(over(new_col, 2), heads) == over(new_row, queries // heads))
        & (mod(over(new_col, 2 * heads), STEPS) <= mod(new_row, STEPS))
    )
    new_slot = jnp.where(new_ok, over(new_col, 2 * heads * STEPS), slots)

    every = range(slots)
    new = new_ref[...]
    new_all = dot_nt(query_ref[...].reshape(slots * queries, HD), new)
    fetch.wait()
    caches = [codes_ref[s] * columns[:, s : s + 1] for s in every]
    scores = [dot_nt(query_ref[s], caches[s]) for s in every]
    scores = [jnp.where(col_token < len_ref[s], scores[s] * SCORE_SCALE, NEGATIVE) for s in every]
    new_scores = [
        jnp.where(new_slot == s, new_all[s * queries : (s + 1) * queries] * SCORE_SCALE, NEGATIVE)
        for s in every
    ]
    top = [top_of(scores[s], new_scores[s]) for s in every]
    weights = [jnp.exp(scores[s] - top[s]) for s in every]
    new_weights = [jnp.exp(new_scores[s] - top[s]) for s in every]
    total = [sum_of(weights[s], new_weights[s]) for s in every]
    new_mixed = dot_nn(jnp.concatenate(new_weights, axis=0).astype(BF16), values_up(new))
    mixed = [
        dot_nn(to_values(weights[s]), caches[s]) + new_mixed[s * queries : (s + 1) * queries]
        for s in every
    ]
    for s in every:
        out_ref[s] = (mixed[s] * (1.0 / total[s])).astype(BF16)


def slots_by_rows(got_ref, tp, order, block_rows):
    chunk_rows = got_ref.shape[2]
    blocks = chunk_rows // block_rows
    rows = [got_ref[k, 0].astype(F32) for k in range(len(order))]
    here = {
        core // tp: jnp.where(x[:1] < EMPTY, 1.0, 0.0)
        for core, x in zip(order, rows)
        if core % tp == 0
    }
    ranks = {
        w: sum([here[v] for v in here if v < w], jnp.zeros((1, HD), F32)) for w in here
    }
    lane = iota((1, HD), 1)
    block = over(lane, block_rows)
    block = jnp.where(mod(lane, 2) == 0, block, -1)
    per_tile = HD // chunk_rows
    tiles = []
    for start in range(0, len(order), per_tile):
        tile = jnp.full((1, HD), -1.0, F32)
        for i in range(per_tile):
            x, rank = rows[start + i], ranks[order[start + i] // tp]
            for b in range(blocks):
                at = b * block_rows
                value = jnp.where(x[at : at + 1] < EMPTY, rank, -1.0)
                tile = jnp.where(block == i * blocks + b, value, tile)
        tiles.append(tile)
    return jnp.concatenate(tiles, axis=1)


def slots_by_matmul(got_ref, tp):
    chunks, _, chunk_rows = got_ref.shape[:3]
    columns = chunks * chunk_rows
    sender_rows = tp * chunk_rows
    piece = min(columns, 256)
    sums = dot_nt(jnp.ones((16, HD), BF16), got_ref[:, 0].reshape(columns, HD))[:8]
    col = iota((8, columns), 1)
    held = sums < EMPTY
    first = jnp.where(held & (mod(col, sender_rows) == 0), 1.0, 0.0).astype(BF16)
    row = over(iota((piece, piece), 0), sender_rows)
    before = jnp.where(row < over(iota((piece, piece), 1), sender_rows), 1.0, 0.0).astype(BF16)
    base = jnp.zeros((8, 1), F32)
    ranks = []
    for p in range(0, columns, piece):
        part = first[:, p : p + piece]
        ranks.append(dot_nn(part, before) + base)
        base = base + jnp.sum(part.astype(F32), axis=1, keepdims=True)
    rank = jnp.concatenate(ranks, axis=1)
    return jnp.where(held & (mod(col, 2) == 0), rank, -1.0)[:1]


def arrival_kernel(
    tp, groups, order, block_rows, got_ref, query_ref, new_ref, done_ref, out_ref, done_hbm, sem
):
    step = pl.program_id(0) if groups > 1 else 0
    hand_on = pltpu.make_async_copy(done_ref, done_hbm, sem)
    if groups > 1:
        pl.when(step == 0)(hand_on.start)
    else:
        hand_on.start()

    chunks, heads, chunk_rows = got_ref.shape[:3]
    slots, _, per_head = query_ref.shape[:3]
    rows = slots * per_head
    columns = chunks * chunk_rows
    every = range(heads)

    caches = [got_ref[:, h].reshape(columns, HD) for h in every]
    queries = [query_ref[:, h].reshape(rows, HD) for h in every]
    new = new_ref[...]
    scores = [dot_nt(queries[h], caches[h]) for h in every]
    new_all = dot_nt(jnp.concatenate(queries, axis=0), new)
    if order is None:
        slot_of = slots_by_matmul(got_ref, tp)
    else:
        slot_of = slots_by_rows(got_ref, tp, order, block_rows)
    first_slot = jnp.float32(step * slots)
    mine = [slot_of == first_slot + a for a in range(slots)]

    new_col = iota((rows, new.shape[0]), 1)
    new_row = iota((rows, new.shape[0]), 0)
    new_here = (
        (mod(new_col, 2) == 0)
        & (over(new_col, 2 * heads * STEPS) == over(new_row, per_head))
        & (mod(over(new_col, 2 * heads), STEPS) <= mod(new_row, STEPS))
    )
    new_head = jnp.where(new_here, mod(over(new_col, 2), heads), heads)

    scores = [
        jnp.concatenate(
            [
                jnp.where(mine[a], scores[h][a * per_head : (a + 1) * per_head] * SCORE_SCALE, NEGATIVE)
                for a in range(slots)
            ],
            axis=0,
        )
        for h in every
    ]
    new_scores = [
        jnp.where(new_head == h, new_all[h * rows : (h + 1) * rows] * SCORE_SCALE, NEGATIVE)
        for h in every
    ]
    top = [top_of(scores[h], new_scores[h]) for h in every]
    weights = [jnp.exp(scores[h] - top[h]) for h in every]
    new_weights = [jnp.exp(new_scores[h] - top[h]) for h in every]
    total = [sum_of(weights[h], new_weights[h]) for h in every]
    new_mixed = dot_nn(jnp.concatenate(new_weights, axis=0).astype(BF16), values_up(new))
    for h in every:
        mixed = dot_nn(to_values(weights[h]), caches[h]) + new_mixed[h * rows : (h + 1) * rows]
        out_ref[:, h] = (mixed * (1.0 / total[h])).astype(BF16).reshape(slots, per_head, HD)
    if groups > 1:
        pl.when(step == groups - 1)(hand_on.wait)
    else:
        hand_on.wait()


def whole(memory_space=pltpu.VMEM):
    return pl.BlockSpec(memory_space=memory_space)


def in_hbm(x):
    return pltpu.with_memory_space_constraint(x, pltpu.HBM)


def limit(mib):
    return pltpu.CompilerParams(vmem_limit_bytes=mib * 2**20)


def pack(pre_codes, pre_scales, req_dest, req_blocks, peers, tp, order):
    requests, blocks, block_tokens = pre_codes.shape[:3]
    tokens = blocks * block_tokens
    codes = (
        pre_codes.reshape(requests, tokens, 2, KVH, HD)
        .transpose(0, 1, 3, 2, 4)
        .reshape(requests, tokens * KVH * 2, HD)
    )
    scales = pre_scales.reshape(requests, tokens * 2, KVH)
    ins = [req_dest, req_blocks, codes, scales]
    return pl.pallas_call(
        functools.partial(pack_kernel, tp, order, KVH, 2 * block_tokens),
        out_shape=pltpu.VMEM((peers * tp, KVH // tp, tokens * 2, HD), BF16),
        in_specs=[whole(pltpu.HBM)] * len(ins),
        out_specs=whole(),
        scratch_shapes=[
            pltpu.SMEM(req_dest.shape, jnp.int32),
            pltpu.SMEM(req_blocks.shape, jnp.int32),
            pltpu.VMEM(codes.shape, BF16),
            pltpu.VMEM(scales.shape, BF16),
            pltpu.SemaphoreType.DMA((5,)),
        ],
        compiler_params=limit(16),
        name="pack",
    )(*[in_hbm(x) for x in ins])


def cache_rows(codes):
    slots, tokens, _, width = codes.shape
    heads = width // HD
    return (
        codes.reshape(slots, tokens, 2, heads, HD)
        .transpose(0, 1, 3, 2, 4)
        .reshape(slots, tokens * heads * 2, HD)
    )


def query_rows(query):
    slots, steps, width = query.shape
    return query.reshape(slots, steps, width // HD, HD).transpose(0, 2, 1, 3)


def new_rows_of(new):
    slots, steps, pair, width = new.shape
    heads = width // HD
    return (
        new.reshape(slots, steps, pair, heads, HD)
        .transpose(0, 1, 3, 2, 4)
        .reshape(slots * steps * heads * pair, HD)
    )


def from_rows(out, shape):
    slots, steps, width = shape
    return out.reshape(slots, width // HD, steps, HD).transpose(0, 2, 1, 3).reshape(shape)


def resident(codes, res_scales, res_len, res_query, res_new):
    slots, rows = codes.shape[:2]
    heads = res_scales.shape[-1]
    scales = res_scales.transpose(0, 2, 3, 1)
    query = query_rows(res_query).reshape(slots, heads * GROUP * STEPS, HD)
    work = query.shape[0] * query.shape[1] * rows
    return pl.pallas_call(
        resident_kernel,
        out_shape=pltpu.VMEM(query.shape, BF16),
        in_specs=[whole(pltpu.SMEM), whole(pltpu.HBM)] + [whole()] * 3,
        out_specs=whole(),
        scratch_shapes=[pltpu.VMEM(codes.shape, BF16), pltpu.SemaphoreType.DMA],
        cost_estimate=pl.CostEstimate(
            flops=4 * work * HD,
            bytes_accessed=2 * (codes.size + 2 * query.size),
            transcendentals=work,
        ),
        compiler_params=limit(16),
        name="resident",
    )(in_hbm(res_len), in_hbm(codes), scales, query, new_rows_of(res_new))


def arrivals(got, arr_query, arr_new, done, tp, order, block_rows):
    slots, steps, width = arr_query.shape
    heads = width // (HD * GROUP)
    query = query_rows(arr_query).reshape(slots, heads, GROUP * steps, HD)
    new = new_rows_of(arr_new)
    size = max(n for n in range(1, 7) if slots % n == 0)
    groups = slots // size
    small = got.size <= 2**18

    def part(ref, rows):
        if groups == 1:
            return whole()
        return pl.BlockSpec((rows,) + ref.shape[1:], lambda i: (i,) + (0,) * (ref.ndim - 1))

    return pl.pallas_call(
        functools.partial(arrival_kernel, tp, groups, order, block_rows),
        out_shape=[
            jax.ShapeDtypeStruct(query.shape, BF16),
            jax.ShapeDtypeStruct(done.shape, BF16),
        ],
        grid=(groups,) if groups > 1 else (),
        in_specs=[
            whole(),
            part(query, size),
            part(new, new.shape[0] // groups),
            whole(),
        ],
        out_specs=[part(query, size), whole(pltpu.HBM)],
        scratch_shapes=[pltpu.SemaphoreType.DMA],
        compiler_params=limit(16 if small else 48),
        name="arrivals",
    )(got, query, new, done)


def shards(
    pre_codes,
    pre_scales,
    req_dest,
    req_blocks,
    res_codes,
    res_scales,
    res_len,
    res_query,
    res_new,
    arr_query,
    arr_new,
):
    peers = lax.axis_size("wide")
    tp = lax.axis_size("tp")
    order = None
    if peers * tp == 16:
        order = [p ^ 7 for p in range(16)]
    send = pack(pre_codes, pre_scales, req_dest, req_blocks, peers, tp, order)
    got = lax.all_to_all(
        send,
        ("wide", "tp"),
        split_axis=0,
        concat_axis=0,
        tiled=True,
        axis_index_groups=[order or list(range(peers * tp))],
    )
    done = resident(cache_rows(res_codes), res_scales, res_len, res_query, res_new)
    block_rows = 2 * pre_codes.shape[2]
    arr_out, res_out = arrivals(got, arr_query, arr_new, done, tp, order, block_rows)
    return (from_rows(res_out, res_query.shape), from_rows(arr_out, arr_query.shape))


def solution(mesh):
    in_specs = (
        P(("groups", "wide"), None, "tp", None, None),
        P(("groups", "wide"), None, "tp", None, None),
        P(("groups", "wide")),
        P(("groups", "wide")),
        P(("groups", "wide"), None, None, "tp"),
        P(("groups", "wide"), None, None, "tp"),
        P(("groups", "wide")),
        P(("groups", "wide"), None, "tp"),
        P(("groups", "wide"), None, None, "tp"),
        P(("groups", "wide"), None, "tp"),
        P(("groups", "wide"), None, None, "tp"),
    )
    out_specs = (P(("groups", "wide"), None, "tp"), P(("groups", "wide"), None, "tp"))
    return jax.shard_map(shards, mesh=mesh, in_specs=in_specs, out_specs=out_specs, check_vma=False)
```

profile of v0, /device:TPU:0, one launch (start us, length us, event | category | flops | bytes accessed | tf_op | source)
XLA Modules:
  0.0 16.5 jit_solution(6787798872713231741)
XLA Ops:
  0.6 1.7 %pack.1 = bf16[16,2,16,128]{3,2,1,0:T(8,128)(2,1)} custom-call(s32[4]{0:T(128)} %dest_hbm.1, s32[4]{0:T(128)} %blocks_hbm.1, bf16[4,64,128]{2,1,0:T(8,128)(2,1)} %bitcast.48, bf16[4,16,4]{2,1,0:T(8,128)(2,1)} %bitcast.49), custom_call_target="tpu_custom_call" | custom-call | tf_op jit(solution)/shard_map/pack/pallas_call | solution.py:308
  2.3 0.0 copy-start
  2.3 0.0 copy-start.2
  2.3 0.0 copy-start.4
  2.3 7.7 %all-to-all-start = ((bf16[16,2,16,128]{3,2,1,0:T(8,128)(2,1)}), bf16[16,2,16,128]{3,2,1,0:T(8,128)(2,1)S(1)}, u32[]{:S(2)}, u32[]{:S(2)}) async-start(bf16[16,2,16,128]{3,2,1,0:T(8,128)(2,1)} %pack.1), calls=%async_computation | async-start | bytes 262144 | tf_op jit(solution)/shard_map/all_to_all | solution.py:430
  10.1 0.0 copy-done
  10.1 0.0 copy-done.2
  10.1 0.0 copy-done.4
  10.1 0.0 copy-start.1
  10.1 0.0 copy-start.3
  10.1 2.7 %resident.1.done_ref = bf16[8,64,128]{2,1,0:T(8,128)(2,1)S(1)} custom-call(s32[8]{0:T(128)} %len_ref.1, bf16[8,256,128]{2,1,0:T(8,128)(2,1)} %bitcast.47, bf16[8,2,2,64]{3,2,1,0:T(2,128)(2,1)S(1)} %bitcast.46, bf16[8,64,128]{2,1,0:T(8,128)(2,1)S(1)} %bitcast.42, bf16[64,128]{1,0:T(8,128)(2,1)S(1)} %bitcast.44), custom_call_target="tpu_custom_call" | custom-call | flops 67108864 | bytes 786432 | tf_op jit(solution)/shard_map/resident/pallas_call | solution.py:361
  12.8 2.3 %all-to-all-done.got_ref = bf16[16,2,16,128]{3,2,1,0:T(8,128)(2,1)S(1)} async-done(((bf16[16,2,16,128]{3,2,1,0:T(8,128)(2,1)}), bf16[16,2,16,128]{3,2,1,0:T(8,128)(2,1)S(1)}, u32[]{:S(2)}, u32[]{:S(2)}) %all-to-all-start) | async-done | bytes 131104 | tf_op jit(solution)/shard_map/all_to_all | solution.py:430
  15.1 0.0 copy-done.1
  15.1 0.0 copy-done.3
  15.1 1.3 %arrivals.1 = (bf16[6,2,32,128]{3,2,1,0:T(8,128)(2,1)}, bf16[8,64,128]{2,1,0:T(8,128)(2,1)}) custom-call(bf16[16,2,16,128]{3,2,1,0:T(8,128)(2,1)S(1)} %all-to-all-done.got_ref, bf16[6,2,32,128]{3,2,1,0:T(8,128)(2,1)S(1)} %bitcast.43, bf16[48,128]{1,0:T(8,128)(2,1)S(1)} %bitcast.45, bf16[8,64,128]{2,1,0:T(8,128)(2,1)S(1)} %resident.1.done_ref), custom_call_target="tpu_custom_call" | custom-call | tf_op jit(solution)/shard_map/arrivals/pallas_call | solution.py:391
Async XLA Ops:
  2.3 7.8 %copy-start = (bf16[8,2,4096]{2,1,0:T(2,128)(2,1)S(1)}, bf16[8,2,4096]{2,1,0:T(2,128)(2,1)}, u32[]{:S(2)}) copy-start(bf16[8,2,4096]{2,1,0:T(2,128)(2,1)} %param.18) | copy-start | bytes 393220
  2.3 7.8 %copy-start.2 = (bf16[8,2,2,256]{3,2,1,0:T(2,128)(2,1)S(1)}, bf16[8,2,2,256]{3,2,1,0:T(2,128)(2,1)}, u32[]{:S(2)}) copy-start(bf16[8,2,2,256]{3,2,1,0:T(2,128)(2,1)} %param.19) | copy-start | bytes 49156
  2.3 7.8 %copy-start.4 = (bf16[8,64,2,2]{1,3,2,0:T(2,128)(2,1)S(1)}, bf16[8,64,2,2]{1,3,2,0:T(2,128)(2,1)}, u32[]{:S(2)}) copy-start(bf16[8,64,2,2]{1,3,2,0:T(2,128)(2,1)} %param.16) | copy-start | bytes 12292
  2.3 12.8 %all-to-all-start = ((bf16[16,2,16,128]{3,2,1,0:T(8,128)(2,1)}), bf16[16,2,16,128]{3,2,1,0:T(8,128)(2,1)S(1)}, u32[]{:S(2)}, u32[]{:S(2)}) async-start(bf16[16,2,16,128]{3,2,1,0:T(8,128)(2,1)} %pack.1), calls=%async_computation | async-start | bytes 262144 | tf_op jit(solution)/shard_map/all_to_all | solution.py:430
  10.1 5.1 %copy-start.1 = (bf16[6,2,4096]{2,1,0:T(2,128)(2,1)S(1)}, bf16[6,2,4096]{2,1,0:T(2,128)(2,1)}, u32[]{:S(2)}) copy-start(bf16[6,2,4096]{2,1,0:T(2,128)(2,1)} %param.20) | copy-start | bytes 294916
  10.1 5.0 %copy-start.3 = (bf16[6,2,2,256]{3,2,1,0:T(2,128)(2,1)S(1)}, bf16[6,2,2,256]{3,2,1,0:T(2,128)(2,1)}, u32[]{:S(2)}) copy-start(bf16[6,2,2,256]{3,2,1,0:T(2,128)(2,1)} %param.21) | copy-start | bytes 36868
where the time goes:
time: 16.8 us; the launch traced here: 16.5 us
  starting transfers between devices  7.73 us (46%)
  Pallas kernels  5.7 us (34%)
  waiting for transfers between devices  2.32 us (14%)
  between operations  0.71 us (4%)
    all_to_all x1, starting transfers between devices, shards(): lax.all_to_all(send, ('wide', 'tp'), split_axis=0, concat_axis=0, tiled=T...  7.73 us
    pallas_call x1, Pallas kernels, resident(): pl.pallas_call(resident_kernel, out_shape=pltpu.VMEM(query.shape, BF16),...  2.7 us
    all_to_all x1, waiting for transfers between devices, shards(): lax.all_to_all(send, ('wide', 'tp'), split_axis=0, concat_axis=0, tiled=T...  2.32 us
    pallas_call x1, Pallas kernels, pack(): pl.pallas_call(functools.partial(pack_kernel, tp, order, KVH, 2 * block_t...  1.66 us
    pallas_call x1, Pallas kernels, arrivals(): pl.pallas_call(functools.partial(arrival_kernel, tp, groups, order, block...  1.34 us
  transfers between devices with their start and end apart: 1, of which 1 were waited for; matrix products, arithmetic and copies ran while one was open for 0% of the time, Pallas kernels for 16%

commit v1 on v0

--- a/solution.py
+++ b/solution.py
@@ -425,7 +425,7 @@
     tp = lax.axis_size("tp")
     order = None
     if peers * tp == 16:
-        order = [p ^ 7 for p in range(16)]
+        order = [(p & 1 | p >> 2 & 2 | p << 1 & 12) ^ 11 for p in range(16)]
     send = pack(pre_codes, pre_scales, req_dest, req_blocks, peers, tp, order)
     got = lax.all_to_all(
         send,

time: 16.8 us -> 16.6 us (0.988)
  waiting for transfers between devices: 2.32 us -> 1.93 us
  starting transfers between devices: 7.73 us -> 7.96 us
    all_to_all x1, waiting for transfers between devices: 2.32 us -> 1.93 us  [shards(): lax.all_to_all(send, ('wide', 'tp'), split_axis=0, concat_axis=0, tiled=T...]
    all_to_all x1, starting transfers between devices: 7.73 us -> 7.96 us  [shards(): lax.all_to_all(send, ('wide', 'tp'), split_axis=0, concat_axis=0, tiled=T...]
  transfers between devices with their start and end apart: 1 -> 1, of which waited for: 1 -> 1; matrix products, arithmetic and copies ran while one was open for 0% -> 0% of each run, Pallas kernels for 16% -> 17%
where the time goes in v1:
time: 16.6 us; the launch traced here: 16.3 us
  starting transfers between devices  7.96 us (48%)
  Pallas kernels  5.7 us (34%)
  waiting for transfers between devices  1.93 us (12%)
  between operations  0.71 us (4%)
    all_to_all x1, starting transfers between devices, shards(): lax.all_to_all(send, ('wide', 'tp'), split_axis=0, concat_axis=0, tiled=T...  7.96 us
    pallas_call x1, Pallas kernels, resident(): pl.pallas_call(resident_kernel, out_shape=pltpu.VMEM(query.shape, BF16),...  2.7 us
    all_to_all x1, waiting for transfers between devices, shards(): lax.all_to_all(send, ('wide', 'tp'), split_axis=0, concat_axis=0, tiled=T...  1.93 us
    pallas_call x1, Pallas kernels, pack(): pl.pallas_call(functools.partial(pack_kernel, tp, order, KVH, 2 * block_t...  1.66 us
    pallas_call x1, Pallas kernels, arrivals(): pl.pallas_call(functools.partial(arrival_kernel, tp, groups, order, block...  1.34 us
  transfers between devices with their start and end apart: 1, of which 1 were waited for; matrix products, arithmetic and copies ran while one was open for 0% of the time, Pallas kernels for 17%

profile of v1, /device:TPU:0, one launch (start us, length us, event | category | flops | bytes accessed | tf_op | source)
XLA Modules:
  0.0 16.3 jit_solution(8254552931458945254)
XLA Ops:
  0.6 1.7 %pack.1 = bf16[16,2,16,128]{3,2,1,0:T(8,128)(2,1)} custom-call(s32[4]{0:T(128)} %dest_hbm.1, s32[4]{0:T(128)} %blocks_hbm.1, bf16[4,64,128]{2,1,0:T(8,128)(2,1)} %bitcast.48, bf16[4,16,4]{2,1,0:T(8,128)(2,1)} %bitcast.49), custom_call_target="tpu_custom_call" | custom-call | tf_op jit(solution)/shard_map/pack/pallas_call | solution.py:308
  2.3 0.0 copy-start
  2.3 0.0 copy-start.2
  2.3 0.0 copy-start.4
  2.3 8.0 %all-to-all-start = ((bf16[16,2,16,128]{3,2,1,0:T(8,128)(2,1)}), bf16[16,2,16,128]{3,2,1,0:T(8,128)(2,1)S(1)}, u32[]{:S(2)}, u32[]{:S(2)}) async-start(bf16[16,2,16,128]{3,2,1,0:T(8,128)(2,1)} %pack.1), calls=%async_computation | async-start | bytes 262144 | tf_op jit(solution)/shard_map/all_to_all | solution.py:430
  10.3 0.0 copy-done
  10.3 0.0 copy-done.2
  10.3 0.0 copy-done.4
  10.3 0.0 copy-start.1
  10.3 0.0 copy-start.3
  10.3 2.7 %resident.1.done_ref = bf16[8,64,128]{2,1,0:T(8,128)(2,1)S(1)} custom-call(s32[8]{0:T(128)} %len_ref.1, bf16[8,256,128]{2,1,0:T(8,128)(2,1)} %bitcast.47, bf16[8,2,2,64]{3,2,1,0:T(2,128)(2,1)S(1)} %bitcast.46, bf16[8,64,128]{2,1,0:T(8,128)(2,1)S(1)} %bitcast.42, bf16[64,128]{1,0:T(8,128)(2,1)S(1)} %bitcast.44), custom_call_target="tpu_custom_call" | custom-call | flops 67108864 | bytes 786432 | tf_op jit(solution)/shard_map/resident/pallas_call | solution.py:361
  13.0 1.9 %all-to-all-done.got_ref = bf16[16,2,16,128]{3,2,1,0:T(8,128)(2,1)S(1)} async-done(((bf16[16,2,16,128]{3,2,1,0:T(8,128)(2,1)}), bf16[16,2,16,128]{3,2,1,0:T(8,128)(2,1)S(1)}, u32[]{:S(2)}, u32[]{:S(2)}) %all-to-all-start) | async-done | bytes 131104 | tf_op jit(solution)/shard_map/all_to_all | solution.py:430
  15.0 0.0 copy-done.1
  15.0 0.0 copy-done.3
  15.0 1.3 %arrivals.1 = (bf16[6,2,32,128]{3,2,1,0:T(8,128)(2,1)}, bf16[8,64,128]{2,1,0:T(8,128)(2,1)}) custom-call(bf16[16,2,16,128]{3,2,1,0:T(8,128)(2,1)S(1)} %all-to-all-done.got_ref, bf16[6,2,32,128]{3,2,1,0:T(8,128)(2,1)S(1)} %bitcast.43, bf16[48,128]{1,0:T(8,128)(2,1)S(1)} %bitcast.45, bf16[8,64,128]{2,1,0:T(8,128)(2,1)S(1)} %resident.1.done_ref), custom_call_target="tpu_custom_call" | custom-call | tf_op jit(solution)/shard_map/arrivals/pallas_call | solution.py:391
Async XLA Ops:
  2.3 8.0 %copy-start = (bf16[8,2,4096]{2,1,0:T(2,128)(2,1)S(1)}, bf16[8,2,4096]{2,1,0:T(2,128)(2,1)}, u32[]{:S(2)}) copy-start(bf16[8,2,4096]{2,1,0:T(2,128)(2,1)} %param.18) | copy-start | bytes 393220
  2.3 8.0 %copy-start.2 = (bf16[8,2,2,256]{3,2,1,0:T(2,128)(2,1)S(1)}, bf16[8,2,2,256]{3,2,1,0:T(2,128)(2,1)}, u32[]{:S(2)}) copy-start(bf16[8,2,2,256]{3,2,1,0:T(2,128)(2,1)} %param.19) | copy-start | bytes 49156
  2.3 8.0 %copy-start.4 = (bf16[8,64,2,2]{1,3,2,0:T(2,128)(2,1)S(1)}, bf16[8,64,2,2]{1,3,2,0:T(2,128)(2,1)}, u32[]{:S(2)}) copy-start(bf16[8,64,2,2]{1,3,2,0:T(2,128)(2,1)} %param.16) | copy-start | bytes 12292
  2.3 12.6 %all-to-all-start = ((bf16[16,2,16,128]{3,2,1,0:T(8,128)(2,1)}), bf16[16,2,16,128]{3,2,1,0:T(8,128)(2,1)S(1)}, u32[]{:S(2)}, u32[]{:S(2)}) async-start(bf16[16,2,16,128]{3,2,1,0:T(8,128)(2,1)} %pack.1), calls=%async_computation | async-start | bytes 262144 | tf_op jit(solution)/shard_map/all_to_all | solution.py:430
  10.3 4.7 %copy-start.1 = (bf16[6,2,4096]{2,1,0:T(2,128)(2,1)S(1)}, bf16[6,2,4096]{2,1,0:T(2,128)(2,1)}, u32[]{:S(2)}) copy-start(bf16[6,2,4096]{2,1,0:T(2,128)(2,1)} %param.20) | copy-start | bytes 294916
  10.3 4.7 %copy-start.3 = (bf16[6,2,2,256]{3,2,1,0:T(2,128)(2,1)S(1)}, bf16[6,2,2,256]{3,2,1,0:T(2,128)(2,1)}, u32[]{:S(2)}) copy-start(bf16[6,2,2,256]{3,2,1,0:T(2,128)(2,1)} %param.21) | copy-start | bytes 36868

commit v2 on v1

--- a/solution.py
+++ b/solution.py
@@ -425,7 +425,7 @@
     tp = lax.axis_size("tp")
     order = None
     if peers * tp == 16:
-        order = [(p & 1 | p >> 2 & 2 | p << 1 & 12) ^ 11 for p in range(16)]
+        order = [(11 - p) % 16 for p in range(16)]
     send = pack(pre_codes, pre_scales, req_dest, req_blocks, peers, tp, order)
     got = lax.all_to_all(
         send,

time: 16.6 us -> 16.1 us (0.970)
  waiting for transfers between devices: 1.93 us -> 1.43 us
    all_to_all x1, waiting for transfers between devices: 1.93 us -> 1.43 us  [shards(): lax.all_to_all(send, ('wide', 'tp'), split_axis=0, concat_axis=0, tiled=T...]
where the time goes in v2:
time: 16.1 us; the launch traced here: 15.8 us
  starting transfers between devices  7.94 us (49%)
  Pallas kernels  5.69 us (35%)
  waiting for transfers between devices  1.43 us (9%)
  between operations  0.71 us (4%)
    all_to_all x1, starting transfers between devices, shards(): lax.all_to_all(send, ('wide', 'tp'), split_axis=0, concat_axis=0, tiled=T...  7.94 us
    pallas_call x1, Pallas kernels, resident(): pl.pallas_call(resident_kernel, out_shape=pltpu.VMEM(query.shape, BF16),...  2.7 us
    pallas_call x1, Pallas kernels, pack(): pl.pallas_call(functools.partial(pack_kernel, tp, order, KVH, 2 * block_t...  1.66 us
    all_to_all x1, waiting for transfers between devices, shards(): lax.all_to_all(send, ('wide', 'tp'), split_axis=0, concat_axis=0, tiled=T...  1.43 us
    pallas_call x1, Pallas kernels, arrivals(): pl.pallas_call(functools.partial(arrival_kernel, tp, groups, order, block...  1.34 us
  transfers between devices with their start and end apart: 1, of which 1 were waited for; matrix products, arithmetic and copies ran while one was open for 0% of the time, Pallas kernels for 17%

profile of v2, /device:TPU:0, one launch (start us, length us, event | category | flops | bytes accessed | tf_op | source)
XLA Modules:
  0.0 15.8 jit_solution(3829960948907915841)
XLA Ops:
  0.6 1.7 %pack.1 = bf16[16,2,16,128]{3,2,1,0:T(8,128)(2,1)} custom-call(s32[4]{0:T(128)} %dest_hbm.1, s32[4]{0:T(128)} %blocks_hbm.1, bf16[4,64,128]{2,1,0:T(8,128)(2,1)} %bitcast.48, bf16[4,16,4]{2,1,0:T(8,128)(2,1)} %bitcast.49), custom_call_target="tpu_custom_call" | custom-call | tf_op jit(solution)/shard_map/pack/pallas_call | solution.py:308
  2.3 0.0 copy-start
  2.3 0.0 copy-start.2
  2.3 0.0 copy-start.4
  2.3 7.9 %all-to-all-start = ((bf16[16,2,16,128]{3,2,1,0:T(8,128)(2,1)}), bf16[16,2,16,128]{3,2,1,0:T(8,128)(2,1)S(1)}, u32[]{:S(2)}, u32[]{:S(2)}) async-start(bf16[16,2,16,128]{3,2,1,0:T(8,128)(2,1)} %pack.1), calls=%async_computation | async-start | bytes 262144 | tf_op jit(solution)/shard_map/all_to_all | solution.py:430
  10.3 0.0 copy-done
  10.3 0.0 copy-done.2
  10.3 0.0 copy-done.4
  10.3 0.0 copy-start.1
  10.3 0.0 copy-start.3
  10.3 2.7 %resident.1.done_ref = bf16[8,64,128]{2,1,0:T(8,128)(2,1)S(1)} custom-call(s32[8]{0:T(128)} %len_ref.1, bf16[8,256,128]{2,1,0:T(8,128)(2,1)} %bitcast.47, bf16[8,2,2,64]{3,2,1,0:T(2,128)(2,1)S(1)} %bitcast.46, bf16[8,64,128]{2,1,0:T(8,128)(2,1)S(1)} %bitcast.42, bf16[64,128]{1,0:T(8,128)(2,1)S(1)} %bitcast.44), custom_call_target="tpu_custom_call" | custom-call | flops 67108864 | bytes 786432 | tf_op jit(solution)/shard_map/resident/pallas_call | solution.py:361
  13.0 1.4 %all-to-all-done.got_ref = bf16[16,2,16,128]{3,2,1,0:T(8,128)(2,1)S(1)} async-done(((bf16[16,2,16,128]{3,2,1,0:T(8,128)(2,1)}), bf16[16,2,16,128]{3,2,1,0:T(8,128)(2,1)S(1)}, u32[]{:S(2)}, u32[]{:S(2)}) %all-to-all-start) | async-done | bytes 131104 | tf_op jit(solution)/shard_map/all_to_all | solution.py:430
  14.5 0.0 copy-done.1
  14.5 0.0 copy-done.3
  14.5 1.3 %arrivals.1 = (bf16[6,2,32,128]{3,2,1,0:T(8,128)(2,1)}, bf16[8,64,128]{2,1,0:T(8,128)(2,1)}) custom-call(bf16[16,2,16,128]{3,2,1,0:T(8,128)(2,1)S(1)} %all-to-all-done.got_ref, bf16[6,2,32,128]{3,2,1,0:T(8,128)(2,1)S(1)} %bitcast.43, bf16[48,128]{1,0:T(8,128)(2,1)S(1)} %bitcast.45, bf16[8,64,128]{2,1,0:T(8,128)(2,1)S(1)} %resident.1.done_ref), custom_call_target="tpu_custom_call" | custom-call | tf_op jit(solution)/shard_map/arrivals/pallas_call | solution.py:391
Async XLA Ops:
  2.3 8.0 %copy-start = (bf16[8,2,4096]{2,1,0:T(2,128)(2,1)S(1)}, bf16[8,2,4096]{2,1,0:T(2,128)(2,1)}, u32[]{:S(2)}) copy-start(bf16[8,2,4096]{2,1,0:T(2,128)(2,1)} %param.18) | copy-start | bytes 393220
  2.3 8.0 %copy-start.2 = (bf16[8,2,2,256]{3,2,1,0:T(2,128)(2,1)S(1)}, bf16[8,2,2,256]{3,2,1,0:T(2,128)(2,1)}, u32[]{:S(2)}) copy-start(bf16[8,2,2,256]{3,2,1,0:T(2,128)(2,1)} %param.19) | copy-start | bytes 49156
  2.3 8.0 %copy-start.4 = (bf16[8,64,2,2]{1,3,2,0:T(2,128)(2,1)S(1)}, bf16[8,64,2,2]{1,3,2,0:T(2,128)(2,1)}, u32[]{:S(2)}) copy-start(bf16[8,64,2,2]{1,3,2,0:T(2,128)(2,1)} %param.16) | copy-start | bytes 12292
  2.3 12.1 %all-to-all-start = ((bf16[16,2,16,128]{3,2,1,0:T(8,128)(2,1)}), bf16[16,2,16,128]{3,2,1,0:T(8,128)(2,1)S(1)}, u32[]{:S(2)}, u32[]{:S(2)}) async-start(bf16[16,2,16,128]{3,2,1,0:T(8,128)(2,1)} %pack.1), calls=%async_computation | async-start | bytes 262144 | tf_op jit(solution)/shard_map/all_to_all | solution.py:430
  10.3 4.2 %copy-start.1 = (bf16[6,2,4096]{2,1,0:T(2,128)(2,1)S(1)}, bf16[6,2,4096]{2,1,0:T(2,128)(2,1)}, u32[]{:S(2)}) copy-start(bf16[6,2,4096]{2,1,0:T(2,128)(2,1)} %param.20) | copy-start | bytes 294916
  10.3 4.2 %copy-start.3 = (bf16[6,2,2,256]{3,2,1,0:T(2,128)(2,1)S(1)}, bf16[6,2,2,256]{3,2,1,0:T(2,128)(2,1)}, u32[]{:S(2)}) copy-start(bf16[6,2,2,256]{3,2,1,0:T(2,128)(2,1)} %param.21) | copy-start | bytes 36868
